TPU v7x, 32 devices: a whole 2x2x4 slice. The times are simulated.
32 devices in a mesh: dom: 8 (over z, core), rep: 4 (over y, x).
Axes of the slice: x: 2, y: 2, z: 4, core: 2. Of those that a mesh axis runs over, the one named last changes fastest.
Arguments:
- features: bfloat16 [8192, 512], P(('dom', 'rep')), may hold values from -6 to 6
- local_counts: int32 [8192, 256], P(('dom', 'rep')), may hold values from 0 to 3, as said below
- remote_counts: int32 [128, 128, 128], P(('dom', 'rep')), may hold values from 0 to 3, as said below
- remote_dest: int32 [32, 4], P(('dom', 'rep')), may hold values from 0 to 1
- send_block: int32 [32, 4], P(('dom', 'rep')), may hold values from 0 to 1
- halo_counts: int32 [64, 128, 128], P(('dom', 'rep')), may hold values from 0 to 3, as said below
- halo_dest: int32 [32, 2], P(('dom', 'rep')), may hold values from 0 to 1
- export_block: int32 [32, 1], P(('dom', 'rep')), may hold values from 0 to 1
- w_self: bfloat16 [512, 512], replicated, may hold values from -0.25 to 0.25
- w_neigh: bfloat16 [512, 512], replicated, may hold values from -0.25 to 0.25
- cotangent: bfloat16 [8192, 512], P(('dom', 'rep')), may hold values from -6 to 6
Outputs:
- output: bfloat16 [8192, 512], P(('dom', 'rep'))
- feature_grads: bfloat16 [8192, 512], P(('dom', 'rep'))
- self_grads: float32 [512, 512], replicated
- neigh_grads: float32 [512, 512], replicated
Inputs may be any that keep to these rules, and one draw needn't show every extreme that they name: `local_counts`: edge counts of one destination row are 0 for isolated nodes and otherwise at most that row's level, a level of 1 to 3. `remote_counts`: as local_counts, with the level of the destination row. `halo_counts`: as local_counts; the entries for the previous partition of partition 0 and the next partition of the last partition are zero.
All inputs are finite; a program needn't handle non-finite values.
Results may differ from a plain program's by a relative error of at most 0.0051.
Values may be sent and summed in bfloat16 or wider, within the bound.
A program may use at most 64 MiB of HBM per device.

v0:
```python
import math

import jax
import jax.numpy as jnp
from jax import lax
from jax.sharding import PartitionSpec as P

BLK = 128


def with_halo(cells, sides, width):
    for axis, dim in sides:
        count = lax.axis_size(axis)
        ends = count - 1
        head = lax.slice_in_dim(cells, 0, width, axis=dim)
        tail = lax.slice_in_dim(cells, cells.shape[dim] - width, cells.shape[dim], axis=dim)
        cells = jnp.concatenate(
            [
                lax.ppermute(tail, axis, [(i, (i + 1) % count) for i in range(ends)]),
                cells,
                lax.ppermute(head, axis, [((i + 1) % count, i) for i in range(ends)]),
            ],
            axis=dim,
        )
    return cells


def placed_counts(hot_bf, counts_bf):
    blocks = hot_bf.shape[1]
    sources = counts_bf.shape[0]
    width = counts_bf.shape[1]
    spread = jnp.einsum("qb,qij->biqj", hot_bf, counts_bf)
    return spread.reshape(blocks * width, sources * width)


def body(
    features,
    local_counts,
    remote_counts,
    remote_dest,
    send_block,
    halo_counts,
    halo_dest,
    export_block,
    w_self,
    w_neigh,
    cotangent,
):
    row_count = features.shape[0]
    feature_width = features.shape[1]
    blocks = row_count // BLK
    group_size = lax.axis_size("rep")
    domain_size = lax.axis_size("dom")
    highest = lax.Precision.HIGHEST
    scale = 1.0 / math.sqrt(row_count * group_size * domain_size)
    feat_blocks = features.reshape(blocks, BLK, feature_width)
    block_ids = jnp.arange(blocks, dtype=jnp.int32)
    remote_hot = (remote_dest[0][:, None] == block_ids[None, :]).astype(jnp.float32)
    send_hot = (send_block[0][:, None] == block_ids[None, :]).astype(jnp.float32)
    halo_hot = (halo_dest[0][:, None] == block_ids[None, :]).astype(jnp.float32)
    export_hot = (export_block[0][:, None] == block_ids[None, :]).astype(jnp.float32)[0]
    outgoing = jnp.take(feat_blocks, send_block[0], axis=0)
    arrived = lax.all_to_all(outgoing, "rep", split_axis=0, concat_axis=0, tiled=True)
    exported = jnp.take(feat_blocks, export_block[0], axis=0)
    padded = with_halo(exported, (("dom", 0),), 1)
    beside = jnp.stack([padded[0], padded[2]])
    local_bf = local_counts.astype(jnp.bfloat16)
    remote_bf = remote_counts.astype(jnp.bfloat16)
    halo_bf = halo_counts.astype(jnp.bfloat16)
    remote_matrix = placed_counts(remote_hot.astype(jnp.bfloat16), remote_bf)
    halo_matrix = placed_counts(halo_hot.astype(jnp.bfloat16), halo_bf)
    summed = jnp.dot(local_bf, features, preferred_element_type=jnp.float32)
    summed = summed + jnp.dot(
        remote_matrix, arrived.reshape(-1, feature_width), preferred_element_type=jnp.float32
    )
    summed = summed + jnp.dot(
        halo_matrix, beside.reshape(-1, feature_width), preferred_element_type=jnp.float32
    )
    degree = jnp.sum(local_counts, axis=1).astype(jnp.float32)
    degree = degree + jnp.einsum(
        "qb,qi->bi",
        remote_hot,
        jnp.sum(remote_counts, axis=2).astype(jnp.float32),
        precision=highest,
    ).reshape(row_count)
    degree = degree + jnp.einsum(
        "qb,qi->bi", halo_hot, jnp.sum(halo_counts, axis=2).astype(jnp.float32), precision=highest
    ).reshape(row_count)
    denom = jnp.maximum(degree, 1.0)
    neighbour_mean = (summed / denom[:, None]).astype(jnp.bfloat16)
    linear = jnp.dot(features, w_self, preferred_element_type=jnp.float32) + jnp.dot(
        neighbour_mean, w_neigh, preferred_element_type=jnp.float32
    )
    output, pullback = jax.vjp(jax.nn.gelu, linear)
    (linear_grad,) = pullback(cotangent.astype(jnp.float32))
    linear_grad = linear_grad.astype(jnp.bfloat16)
    self_part = (
        jnp.einsum("rf,rg->fg", features, linear_grad, preferred_element_type=jnp.float32) * scale
    )
    neigh_part = (
        jnp.einsum("rf,rg->fg", neighbour_mean, linear_grad, preferred_element_type=jnp.float32)
        * scale
    )
    group_self, group_neigh = lax.psum((self_part, neigh_part), "rep")
    self_grads, neigh_grads = lax.psum((group_self, group_neigh), "dom")
    mean_grad = (
        jnp.dot(linear_grad, w_neigh.T, preferred_element_type=jnp.float32) / denom[:, None]
    ).astype(jnp.bfloat16)
    grad_blocks = mean_grad.reshape(blocks, BLK, feature_width)
    input_grad = jnp.dot(linear_grad, w_self.T, preferred_element_type=jnp.float32)
    input_grad = input_grad + jnp.einsum(
        "ij,if->jf", local_bf, mean_grad, preferred_element_type=jnp.float32
    )
    input_blocks = input_grad.reshape(blocks, BLK, feature_width)
    picked = jnp.take(grad_blocks, remote_dest[0], axis=0)
    edge_terms = jnp.einsum(
        "qij,qif->qjf", remote_bf, picked, preferred_element_type=jnp.float32
    ).astype(jnp.bfloat16)
    returned = lax.all_to_all(edge_terms, "rep", split_axis=0, concat_axis=0, tiled=True)
    input_blocks = input_blocks + jnp.einsum(
        "qb,qjf->bjf", send_hot.astype(jnp.bfloat16), returned, preferred_element_type=jnp.float32
    )
    halo_picked = jnp.take(grad_blocks, halo_dest[0], axis=0)
    halo_terms = jnp.einsum(
        "qij,qif->qjf", halo_bf, halo_picked, preferred_element_type=jnp.float32
    ).astype(jnp.bfloat16)
    gathered = with_halo(halo_terms[None], (("dom", 0),), 1)
    incoming = gathered[0, 1].astype(jnp.float32) + gathered[2, 0].astype(jnp.float32)
    input_blocks = input_blocks + export_hot[:, None, None] * incoming[None, :, :]
    feature_grads = input_blocks.reshape(row_count, feature_width).astype(jnp.bfloat16)
    return (output.astype(jnp.bfloat16), feature_grads, self_grads, neigh_grads)


def solution(mesh):
    return jax.shard_map(
        body,
        mesh=mesh,
        in_specs=(
            P(("dom", "rep"), None),
            P(("dom", "rep"), None),
            P(("dom", "rep"), None, None),
            P(("dom", "rep"), None),
            P(("dom", "rep"), None),
            P(("dom", "rep"), None, None),
            P(("dom", "rep"), None),
            P(("dom", "rep"), None),
            P(),
            P(),
            P(("dom", "rep"), None),
        ),
        out_specs=(P(("dom", "rep"), None), P(("dom", "rep"), None), P(), P()),
        check_vma=False,
    )
```

profile of v0, /device:TPU:1, one launch (start us, length us, event | category | flops | bytes accessed | tf_op | source)
XLA Modules:
  0.0 180.3 jit_solution(13436035874707609212)
XLA Ops:
  7.9 0.9 dynamic-slice_select_fusion
  8.9 2.0 %collective-permute-start.1 = (bf16[1,128,512]{2,1,0:T(8,128)(2,1)S(1)}, bf16[1,128,512]{2,1,0:T(8,128)(2,1)}, u32[]{:S(2)}, u32[]{:S(2)}) collective-permute-start(bf16[1,128,512]{2,1,0:T(8,128)(2,1)S(1)} %dynamic-slice_select_fusion), channel_id=1, source_target_pairs={{4,0},{8,4},{12,8},{16,12},{20,16},{24,20},{28,24},{5,1},{9,5},{13... | collective-permute-start | bytes 393224 | tf_op jit(solution)/shard_map/ppermute | solution.py:21
  10.8 4.6 %collective-permute-start = (bf16[1,128,512]{2,1,0:T(8,128)(2,1)S(1)}, bf16[1,128,512]{2,1,0:T(8,128)(2,1)}, u32[]{:S(2)}, u32[]{:S(2)}) collective-permute-start(bf16[1,128,512]{2,1,0:T(8,128)(2,1)S(1)} %dynamic-slice_select_fusion), channel_id=1, source_target_pairs={{0,4},{4,8},{8,12},{12,16},{16,20},{20,24},{24,28},{1,5},{5,9},{9,... | collective-permute-start | bytes 393224 | tf_op jit(solution)/shard_map/ppermute | solution.py:19
  15.4 0.6 gather_fusion.1
  16.0 0.9 broadcast_select_fusion
  17.0 3.6 %all-to-all-start = ((bf16[4,128,512]{2,1,0:T(8,128)(2,1)}), bf16[4,128,512]{2,1,0:T(8,128)(2,1)S(1)}, u32[]{:S(2)}, u32[]{:S(2)}) async-start(bf16[4,128,512]{2,1,0:T(8,128)(2,1)} %broadcast_select_fusion), calls=%async_computation | async-start | bytes 1048576 | tf_op jit(solution)/shard_map/all_to_all | solution.py:63
  23.1 1.0 pad_maximum_fusion
  24.1 4.4 %all-to-all-done = bf16[4,128,512]{2,1,0:T(8,128)(2,1)S(1)} async-done(((bf16[4,128,512]{2,1,0:T(8,128)(2,1)}), bf16[4,128,512]{2,1,0:T(8,128)(2,1)S(1)}, u32[]{:S(2)}, u32[]{:S(2)}) %all-to-all-start) | async-done | bytes 524320 | tf_op jit(solution)/shard_map/all_to_all | solution.py:63
  29.3 0.7 copy-done.8
  30.0 1.4 fusion.12
  31.4 1.3 convolution_multiply_fusion
  32.7 1.3 fusion
  35.4 2.9 %collective-permute-start.3 = (bf16[1,2,128,512]{2,3,1,0:T(8,128)(2,1)S(1)}, bf16[1,2,128,512]{2,3,1,0:T(8,128)(2,1)S(1)}, u32[]{:S(2)}, u32[]{:S(2)}) collective-permute-start(bf16[1,2,128,512]{2,3,1,0:T(8,128)(2,1)S(1)} %fusion.6), channel_id=1, source_target_pairs={{4,0},{8,4},{12,8},{16,12},{20,16},{24,20},{28,24},{5,1},{9,5},{13... | collective-permute-start | bytes 786440 | tf_op jit(solution)/shard_map/ppermute | solution.py:21
  38.3 3.1 %collective-permute-start.2 = (bf16[1,2,128,512]{2,3,1,0:T(8,128)(2,1)S(1)}, bf16[1,2,128,512]{2,3,1,0:T(8,128)(2,1)}, u32[]{:S(2)}, u32[]{:S(2)}) collective-permute-start(bf16[1,2,128,512]{2,3,1,0:T(8,128)(2,1)S(1)} %fusion.6), channel_id=1, source_target_pairs={{0,4},{4,8},{8,12},{12,16},{16,20},{20,24},{24,28},{1,5},{5,9},{9,... | collective-permute-start | bytes 786440 | tf_op jit(solution)/shard_map/ppermute | solution.py:19
  41.4 0.6 gather_fusion.2
  42.4 61.2 %all-reduce.7.cloned.1.call-done = (f32[512,512]{0,1:T(8,128)}, f32[512,512]{1,0:T(8,128)}) async-done(((f32[512,512]{0,1:T(8,128)}, f32[512,512]{1,0:T(8,128)}), (f32[512,512]{0,1:T(8,128)}, f32[512,512]{1,0:T(8,128)})) %all-reduce.7.cloned.1.call-update) | async-done | bytes 2097168 | tf_op jit(solution)/shard_map/psum | solution.py:104
  104.0 1.0 copy.38
  105.0 3.5 %all-to-all-start.1 = ((bf16[4,128,512]{2,1,0:T(8,128)(2,1)}), bf16[4,128,512]{2,1,0:T(8,128)(2,1)S(1)}, u32[]{:S(2)}, u32[]{:S(2)}) async-start(bf16[4,128,512]{2,1,0:T(8,128)(2,1)} %copy.38), calls=%async_computation.1 | async-start | bytes 1048576 | tf_op jit(solution)/shard_map/all_to_all | solution.py:119
  108.8 0.9 add_bitcast_fusion
  109.9 6.2 %all-to-all-done.1 = bf16[4,128,512]{2,1,0:T(8,128)(2,1)S(1)} async-done(((bf16[4,128,512]{2,1,0:T(8,128)(2,1)}), bf16[4,128,512]{2,1,0:T(8,128)(2,1)S(1)}, u32[]{:S(2)}, u32[]{:S(2)}) %all-to-all-start.1) | async-done | bytes 524320 | tf_op jit(solution)/shard_map/all_to_all | solution.py:119
  116.6 0.9 fusion.21
  117.4 52.5 %all-reduce.5.cloned.1.call-done = (f32[512,512]{0,1:T(8,128)}, f32[512,512]{1,0:T(8,128)}) async-done(((f32[512,512]{0,1:T(8,128)}, f32[512,512]{1,0:T(8,128)}), (f32[512,512]{0,1:T(8,128)}, f32[512,512]{1,0:T(8,128)})) %all-reduce.5.cloned.1.call-update) | async-done | bytes 2097168 | tf_op jit(solution)/shard_map/psum | solution.py:105
  169.9 2.6 %copy.43 = f32[512,512]{1,0:T(8,128)} copy(f32[512,512]{0,1:T(8,128)} %get-tuple-element.32) | data formatting | bytes 2097152
  172.5 1.0 copy.68
  (62 shorter events, 6.3 us)
Async XLA Ops:
  7.2 22.1 %copy-start = (bf16[512,512]{1,0:T(8,128)(2,1)S(1)}, bf16[512,512]{1,0:T(8,128)(2,1)}, u32[]{:S(2)}) copy-start(bf16[512,512]{1,0:T(8,128)(2,1)} %param.22) | copy-start | bytes 1572868
  7.2 8.3 %copy-start.1 = (bf16[256,512]{1,0:T(8,128)(2,1)S(1)}, bf16[256,512]{1,0:T(8,128)(2,1)}, u32[]{:S(2)}) copy-start(bf16[256,512]{1,0:T(8,128)(2,1)} %param.13) | copy-start | bytes 786436
  7.9 7.5 %copy-start.7 = (s32[1,4]{1,0:T(1,128)S(1)}, s32[1,4]{1,0:T(1,128)}, u32[]{:S(2)}) copy-start(s32[1,4]{1,0:T(1,128)} %param.17) | copy-start | bytes 52
  8.9 14.3 %collective-permute-start.1 = (bf16[1,128,512]{2,1,0:T(8,128)(2,1)S(1)}, bf16[1,128,512]{2,1,0:T(8,128)(2,1)}, u32[]{:S(2)}, u32[]{:S(2)}) collective-permute-start(bf16[1,128,512]{2,1,0:T(8,128)(2,1)S(1)} %dynamic-slice_select_fusion), channel_id=1, source_target_pairs={{4,0},{8,4},{12,8},{16,12},{20,16},{24,20},{28,24},{5,1},{9,5},{13... | collective-permute-start | bytes 393224 | tf_op jit(solution)/shard_map/ppermute | solution.py:21
  10.8 12.3 %collective-permute-start = (bf16[1,128,512]{2,1,0:T(8,128)(2,1)S(1)}, bf16[1,128,512]{2,1,0:T(8,128)(2,1)}, u32[]{:S(2)}, u32[]{:S(2)}) collective-permute-start(bf16[1,128,512]{2,1,0:T(8,128)(2,1)S(1)} %dynamic-slice_select_fusion), channel_id=1, source_target_pairs={{0,4},{4,8},{8,12},{12,16},{16,20},{20,24},{24,28},{1,5},{5,9},{9,... | collective-permute-start | bytes 393224 | tf_op jit(solution)/shard_map/ppermute | solution.py:19
  16.9 3.7 %copy-start.10 = (s32[1,2]{1,0:T(1,128)S(1)}, s32[1,2]{1,0:T(1,128)}, u32[]{:S(2)}) copy-start(s32[1,2]{1,0:T(1,128)} %param.19) | copy-start | bytes 28
  16.9 3.7 %copy-start.9 = (s32[1,4]{1,0:T(1,128)S(1)}, s32[1,4]{1,0:T(1,128)}, u32[]{:S(2)}) copy-start(s32[1,4]{1,0:T(1,128)} %param.16) | copy-start | bytes 52
  16.9 3.7 %copy-start.6 = (s32[2,128,128]{2,1,0:T(8,128)S(1)}, s32[2,128,128]{2,1,0:T(8,128)}, u32[]{:S(2)}) copy-start(s32[2,128,128]{2,1,0:T(8,128)} %param.18) | copy-start | bytes 393220
  17.0 3.9 %copy-start.5 = (s32[4,128,128]{2,1,0:T(8,128)S(1)}, s32[4,128,128]{2,1,0:T(8,128)}, u32[]{:S(2)}) copy-start(s32[4,128,128]{2,1,0:T(8,128)} %param.15) | copy-start | bytes 786436
  17.0 11.5 %all-to-all-start = ((bf16[4,128,512]{2,1,0:T(8,128)(2,1)}), bf16[4,128,512]{2,1,0:T(8,128)(2,1)S(1)}, u32[]{:S(2)}, u32[]{:S(2)}) async-start(bf16[4,128,512]{2,1,0:T(8,128)(2,1)} %broadcast_select_fusion), calls=%async_computation | async-start | bytes 1048576 | tf_op jit(solution)/shard_map/all_to_all | solution.py:63
  20.6 1.0 copy-start.3
  20.6 83.0 %all-reduce.7.cloned.1.call-start = ((), (), s32[]{:S(2)}) async-start(), calls=%async_computation.3 | async-start | bytes 4194304 | tf_op jit(solution)/shard_map/psum | solution.py:104
  21.9 1.0 copy-start.2
  29.0 1.0 copy-start.8
  34.0 135.9 %all-reduce.5.cloned.1.call-start = ((), (), s32[]{:S(2)}) async-start(), calls=%async_computation.2 | async-start | bytes 4194304 | tf_op jit(solution)/shard_map/psum | solution.py:105
  35.4 73.4 %collective-permute-start.3 = (bf16[1,2,128,512]{2,3,1,0:T(8,128)(2,1)S(1)}, bf16[1,2,128,512]{2,3,1,0:T(8,128)(2,1)S(1)}, u32[]{:S(2)}, u32[]{:S(2)}) collective-permute-start(bf16[1,2,128,512]{2,3,1,0:T(8,128)(2,1)S(1)} %fusion.6), channel_id=1, source_target_pairs={{4,0},{8,4},{12,8},{16,12},{20,16},{24,20},{28,24},{5,1},{9,5},{13... | collective-permute-start | bytes 786440 | tf_op jit(solution)/shard_map/ppermute | solution.py:21
  38.3 70.5 %collective-permute-start.2 = (bf16[1,2,128,512]{2,3,1,0:T(8,128)(2,1)S(1)}, bf16[1,2,128,512]{2,3,1,0:T(8,128)(2,1)}, u32[]{:S(2)}, u32[]{:S(2)}) collective-permute-start(bf16[1,2,128,512]{2,3,1,0:T(8,128)(2,1)S(1)} %fusion.6), channel_id=1, source_target_pairs={{0,4},{4,8},{8,12},{12,16},{16,20},{20,24},{24,28},{1,5},{5,9},{9,... | collective-permute-start | bytes 786440 | tf_op jit(solution)/shard_map/ppermute | solution.py:19
  105.0 11.0 %all-to-all-start.1 = ((bf16[4,128,512]{2,1,0:T(8,128)(2,1)}), bf16[4,128,512]{2,1,0:T(8,128)(2,1)S(1)}, u32[]{:S(2)}, u32[]{:S(2)}) async-start(bf16[4,128,512]{2,1,0:T(8,128)(2,1)} %copy.38), calls=%async_computation.1 | async-start | bytes 1048576 | tf_op jit(solution)/shard_map/all_to_all | solution.py:119
  169.9 2.6 %copy-start.4 = (f32[512,512]{1,0:T(8,128)S(1)}, f32[512,512]{1,0:T(8,128)}, u32[]{:S(2)}) copy-start(f32[512,512]{1,0:T(8,128)} %get-tuple-element.45) | copy-start | bytes 3145732
Sparse Core Ops, SparseCore 0:
  34.1 69.4 all-reduce.6
  106.1 63.7 all-reduce.4
where the time goes:
time: 182 us; the launch traced here: 180 us
  waiting for transfers between devices  124 us (68%)
  starting transfers between devices  19.7 us (11%)
  between operations  15.2 us (8%)
  local copies, waits for them, and re-layouts  8.31 us (5%)
  matrix products  7.45 us (4%)
  other arithmetic  5.4 us (3%)
    psum x1, waiting for transfers between devices, body(): group_self, group_neigh = lax.psum((self_part, neigh_part), 'rep')  61.2 us
    psum x1, waiting for transfers between devices, body(): self_grads, neigh_grads = lax.psum((group_self, group_neigh), 'dom')  52.5 us
    ppermute x2, starting transfers between devices, with_halo(): lax.ppermute(tail, axis, [(i, (i + 1) % count) for i in range(ends)])  7.65 us
    all_to_all x1, waiting for transfers between devices, body(): lax.all_to_all(edge_terms, 'rep', split_axis=0, concat_axis=0, tiled=True)  6.17 us
    unnamed x24, local copies, waits for them, and re-layouts  5.28 us
    ppermute x2, starting transfers between devices, with_halo(): lax.ppermute(head, axis, [((i + 1) % count, i) for i in range(ends)])  4.89 us
    all_to_all x1, waiting for transfers between devices, body(): lax.all_to_all(outgoing, 'rep', split_axis=0, concat_axis=0, tiled=True)  4.36 us
  transfers between devices with their start and end apart: 8, of which 4 were waited for; matrix products, arithmetic and copies ran while one was open for 6% of the time, Pallas kernels for 0%

commit v1 on v0

v1 whole, which is shorter than its diff:
```python
import functools
import math

import jax
import jax.numpy as jnp
from jax import lax
from jax.experimental import pallas as pl
from jax.experimental.pallas import tpu as pltpu
from jax.sharding import PartitionSpec as P

BLK = 128
MESH = pl.DeviceIdType.MESH
F32 = jnp.float32
BF16 = jnp.bfloat16


def dot(a, b):
    return jnp.dot(a, b, preferred_element_type=F32)


def dot_t(a, b):
    return lax.dot_general(a, b, (((0,), (0,)), ((), ())), preferred_element_type=F32)


def dot_nt(a, b):
    return lax.dot_general(a, b, (((1,), (1,)), ((), ())), preferred_element_type=F32)


def rows_at(start, size):
    return pl.ds(pl.multiple_of(start, size), size)


def kernel(
    domains, members, pieces, scale,
    feat_h, loc_h, rem_h, rdest_h, send_h, halo_h, hdest_h, exp_h, ws_h, wn_h, cot_h,
    out_h, fg_h, grads_h,
    pair, loc_v, rem_v, halo_v, ws_v, wn_v, cot_v, out_v, fg_v,
    rdest, send, hdest, export,
    outgoing, exported, arrived, beside, adj, acc, lin, lg, mg,
    mate_out, mate_in, own, xy_out, xy_in, zsum, z_out, z_in, grads,
    edge, returned, halo_edge, halo_back,
    in_sem, out_sem,
    f_send, f_recv, h_send, h_recv,
    m_send, m_recv, x_send, x_recv, z_send, z_recv,
    e_send, e_recv, b_send, b_recv,
    gz_send, gz_recv, gx_send, gx_recv, gm_send, gm_recv,
):
    dom = lax.axis_index("dom")
    me = lax.axis_index("rep")
    z = dom // 2
    core = dom % 2
    mate = dom + 1 - 2 * core
    zs = domains // 2
    rows, width = out_v.shape
    blocks = rows // BLK
    chunk = width // members
    piece = chunk // pieces
    peers = [(me + k) % members for k in range(1, members)]
    zpeers = [(z + k) % zs for k in range(1, zs)]
    has_prev = dom > 0
    has_next = dom < domains - 1
    sends = []

    def remote(src, dst, s_sem, r_sem, to):
        return pltpu.make_async_remote_copy(
            src_ref=src, dst_ref=dst, send_sem=s_sem, recv_sem=r_sem,
            device_id=to, device_id_type=MESH,
        )

    def push(*args):
        copy = remote(*args)
        copy.start()
        sends.append(copy)

    barrier = pltpu.get_barrier_semaphore()

    def greet(to):
        pl.semaphore_signal(barrier, inc=1, device_id=to, device_id_type=MESH)

    for q in peers:
        greet((dom, q))
    for j in zpeers:
        greet((j * 2 + core, me))
    greet((mate, me))
    outer = jnp.where(core == 0, dom - 1, dom + 1)
    has_outer = jnp.logical_and(outer >= 0, outer < domains)

    @pl.when(has_outer)
    def _():
        greet((outer, me))

    loads = {}
    for i, (name, src, dst) in enumerate([
        ("feat", feat_h, pair.at[0]), ("send", send_h, send), ("export", exp_h, export),
        ("rdest", rdest_h, rdest), ("hdest", hdest_h, hdest), ("loc", loc_h, loc_v),
        ("rem", rem_h, rem_v), ("halo", halo_h, halo_v), ("ws", ws_h, ws_v),
        ("wn", wn_h, wn_v), ("cot", cot_h, cot_v),
    ]):
        loads[name] = pltpu.make_async_copy(src, dst, in_sem.at[i])
        loads[name].start()

    for name in ("send", "export", "feat"):
        loads[name].wait()

    def picked(index):
        total = jnp.zeros((BLK, width), F32)
        for b in range(blocks):
            total = total + pair[0, b * BLK:(b + 1) * BLK, :].astype(F32) * (index == b).astype(F32)
        return total.astype(BF16)

    for q in peers:
        outgoing[rows_at(q * BLK, BLK), :] = picked(send[0, q])
    arrived[rows_at(me * BLK, BLK), :] = picked(send[0, me])
    exported[...] = picked(export[0, 0])

    pl.semaphore_wait(barrier, len(peers) + len(zpeers) + 1 + has_outer.astype(jnp.int32))

    for q in peers:
        push(
            outgoing.at[rows_at(q * BLK, BLK)], arrived.at[rows_at(me * BLK, BLK)],
            f_send.at[q], f_recv.at[me], (dom, q),
        )

    def exchange(sources, landing, s_sem, r_sem):
        to_prev = remote(sources[0], landing.at[pl.ds(BLK, BLK)], s_sem.at[0], r_sem.at[1], (dom - 1, me))
        to_next = remote(sources[1], landing.at[pl.ds(0, BLK)], s_sem.at[1], r_sem.at[0], (dom + 1, me))
        return to_prev, to_next

    def start_exchange(copies, landing):
        for slot, (there, copy) in enumerate(zip((has_prev, has_next), copies)):
            @pl.when(there)
            def _(copy=copy):
                copy.start()

            @pl.when(jnp.logical_not(there))
            def _(slot=slot):
                landing[pl.ds(slot * BLK, BLK), :] = jnp.zeros((BLK, width), BF16)

    def arrive_exchange(copies):
        to_prev, to_next = copies

        @pl.when(has_prev)
        def _():
            to_next.wait_recv()

        @pl.when(has_next)
        def _():
            to_prev.wait_recv()

    def end_exchange(copies):
        for there, copy in zip((has_prev, has_next), copies):
            @pl.when(there)
            def _(copy=copy):
                copy.wait_send()

    halo_f = exchange((exported, exported), beside, h_send, h_recv)
    start_exchange(halo_f, beside)

    for name in ("rdest", "hdest", "loc", "rem", "halo"):
        loads[name].wait()
    counts = loc_v[...].astype(F32)
    adj[:, :rows] = counts.astype(BF16)
    local_degree = jnp.sum(counts, axis=1, keepdims=True)
    for b in range(blocks):
        total = jnp.zeros((BLK, BLK), F32)
        for q in range(members + 2):
            if q < members:
                here = (rdest[0, q] == b).astype(F32)
                placed = rem_v[q].astype(F32) * here
            else:
                here = (hdest[0, q - members] == b).astype(F32)
                placed = halo_v[q - members].astype(F32) * here
            total = total + placed
            adj[b * BLK:(b + 1) * BLK, rows + q * BLK:rows + (q + 1) * BLK] = placed.astype(BF16)
        degree = jnp.sum(total, axis=1, keepdims=True) + local_degree[b * BLK:(b + 1) * BLK]
        acc[b * BLK:(b + 1) * BLK, :BLK] = jnp.broadcast_to(1.0 / jnp.maximum(degree, 1.0), (BLK, BLK))
    inverse = acc[:, :1]

    acc[...] = dot(adj[:, :rows], pair[0])
    loads["ws"].wait()
    lin[...] = dot(pair[0], ws_v[...])
    loads["wn"].wait()
    loads["cot"].wait()
    arrive_exchange(halo_f)
    acc[...] += dot(adj[:, rows + members * BLK:], beside[...])
    for q in peers:
        slot = arrived.at[rows_at(q * BLK, BLK)]
        remote(slot, slot, f_send.at[q], f_recv.at[q], (dom, q)).wait_recv()
    mean = (acc[...] + dot(adj[:, rows:rows + members * BLK], arrived[...])) * inverse
    pair[1] = mean.astype(BF16)

    x = lin[...] + dot(pair[1], wn_v[...])
    c = math.sqrt(2.0 / math.pi)
    square = x * x
    t = jnp.tanh(c * (x + 0.044715 * (x * square)))
    half = 0.5 * (1.0 + t)
    out_v[...] = (x * half).astype(BF16)
    slope = half + 0.5 * x * (1.0 - t * t) * (c * (1.0 + 3.0 * 0.044715 * square))
    lg[...] = (cot_v[...].astype(F32) * slope).astype(BF16)
    out_copy = pltpu.make_async_copy(out_v, out_h, out_sem.at[0])
    out_copy.start()

    mate_out[...] = dot_t(pair[1 - core], lg[...]).astype(BF16)
    order = peers + [me]
    for q in order:
        at = rows_at(q * chunk, chunk)
        push(mate_out.at[at], mate_in.at[at], m_send.at[q], m_recv.at[q], (mate, me))
    own[...] = dot_t(pair[core], lg[...])

    mg[...] = (dot_nt(lg[...], wn_v[...]) * inverse).astype(BF16)
    edge[...] = dot_t(adj[:, rows:rows + members * BLK], mg[...]).astype(BF16)
    halo_edge[...] = dot_t(adj[:, rows + members * BLK:], mg[...]).astype(BF16)
    returned[rows_at(me * BLK, BLK), :] = edge[rows_at(me * BLK, BLK), :]

    for q in order:
        at = rows_at(q * chunk, chunk)
        remote(mate_out.at[at], mate_in.at[at], m_send.at[q], m_recv.at[q], (mate, me)).wait_recv()
        both = own[at, :] + mate_in[at, :].astype(F32)
        if q is me:
            zsum[...] = both
        else:
            xy_out[at, :] = both.astype(BF16)
            push(xy_out.at[at], xy_in.at[rows_at(me * chunk, chunk)], x_send.at[q], x_recv.at[me], (dom, q))

    for q in peers:
        push(
            edge.at[rows_at(q * BLK, BLK)], returned.at[rows_at(me * BLK, BLK)],
            e_send.at[q], e_recv.at[me], (dom, q),
        )
    halo_b = exchange((halo_edge.at[pl.ds(0, BLK)], halo_edge.at[pl.ds(BLK, BLK)]), halo_back, b_send, b_recv)
    start_exchange(halo_b, halo_back)
    acc[...] = dot_nt(lg[...], ws_v[...]) + dot_t(adj[:, :rows], mg[...])

    for q in peers:
        at = rows_at(q * chunk, chunk)
        remote(xy_out.at[at], xy_in.at[at], x_send.at[q], x_recv.at[q], (dom, q)).wait_recv()
        zsum[...] += xy_in[at, :].astype(F32)

    def place(member, part):
        return rows_at((core * members + member) * chunk + part * piece, piece)

    def z_slot(j):
        return z_in.at[rows_at(j * piece, piece)]

    part = z if pieces > 1 else 0
    for j in zpeers:
        at = rows_at((j if pieces > 1 else 0) * piece, piece)
        to = rows_at(j * piece, piece)
        z_out[to, :] = zsum[at, :].astype(BF16)
        push(z_out.at[to], z_slot(z), z_send.at[j], z_recv.at[z], (j * 2 + core, me))
    z_in[rows_at(z * piece, piece), :] = zsum[rows_at(part * piece, piece), :].astype(BF16)
    for j in zpeers:
        remote(z_slot(j), z_slot(j), z_send.at[j], z_recv.at[j], (j * 2 + core, me)).wait_recv()
    total = z_in[:piece, :].astype(F32)
    for j in range(1, zs):
        total = total + z_in[j * piece:(j + 1) * piece, :].astype(F32)
    grads[place(me, part), :] = (total * scale).astype(BF16)

    def spread(part):
        at = grads.at[place(me, part)]
        for q in peers:
            push(at, at, gx_send.at[q * pieces + part], gx_recv.at[me * pieces + part], (dom, q))
        push(at, at, gm_send.at[me * pieces + part], gm_recv.at[me * pieces + part], (mate, me))

    if pieces > 1:
        at = grads.at[place(me, z)]
        for j in zpeers:
            push(at, at, gz_send.at[j], gz_recv.at[z], (j * 2 + core, me))
    spread(part)
    if pieces > 1:
        for j in zpeers:
            at = grads.at[place(me, j)]
            remote(at, at, gz_send.at[j], gz_recv.at[j], (j * 2 + core, me)).wait_recv()
            spread(j)

    arrive_exchange(halo_b)
    for q in peers:
        slot = returned.at[rows_at(q * BLK, BLK)]
        remote(slot, slot, e_send.at[q], e_recv.at[q], (dom, q)).wait_recv()
    incoming = halo_back[:BLK, :].astype(F32) + halo_back[BLK:, :].astype(F32)
    for b in range(blocks):
        total = acc[b * BLK:(b + 1) * BLK, :] + incoming * (export[0, 0] == b).astype(F32)
        for q in range(members):
            back = returned[q * BLK:(q + 1) * BLK, :].astype(F32)
            total = total + back * (send[0, q] == b).astype(F32)
        fg_v[b * BLK:(b + 1) * BLK, :] = total.astype(BF16)
    fg_copy = pltpu.make_async_copy(fg_v, fg_h, out_sem.at[1])
    fg_copy.start()

    parts = [part] + (zpeers if pieces > 1 else [])
    for j in parts:
        for q in peers:
            at = grads.at[place(q, j)]
            remote(at, at, gx_send.at[q * pieces + j], gx_recv.at[q * pieces + j], (dom, q)).wait_recv()
            push(at, at, gm_send.at[q * pieces + j], gm_recv.at[q * pieces + j], (mate, me))
    for j in parts:
        for q in order:
            at = grads.at[rows_at(((1 - core) * members + q) * chunk + j * piece, piece)]
            remote(at, at, gm_send.at[q * pieces + j], gm_recv.at[q * pieces + j], (mate, me)).wait_recv()
    grads_copy = pltpu.make_async_copy(grads, grads_h, out_sem.at[2])
    grads_copy.start()

    for copy in sends:
        copy.wait_send()
    end_exchange(halo_f)
    end_exchange(halo_b)
    out_copy.wait()
    fg_copy.wait()
    grads_copy.wait()


def body(domains, members, *args):
    features, w_self = args[0], args[8]
    rows, width = features.shape
    zs = domains // 2
    chunk = width // members
    pieces = zs if chunk % (16 * zs) == 0 else 1
    piece = chunk // pieces
    scale = 1.0 / math.sqrt(rows * members * domains)
    any_space = pl.BlockSpec(memory_space=pl.ANY)
    dma = pltpu.SemaphoreType.DMA

    def vmem(*shape, dtype=BF16):
        return pltpu.VMEM(shape, dtype)

    scratch = [
        vmem(2, rows, width),
        vmem(rows, rows, dtype=jnp.int32),
        vmem(members, BLK, BLK, dtype=jnp.int32),
        vmem(2, BLK, BLK, dtype=jnp.int32),
        vmem(width, width), vmem(width, width), vmem(rows, width),
        vmem(rows, width), vmem(rows, width),
        pltpu.SMEM((1, members), jnp.int32), pltpu.SMEM((1, members), jnp.int32),
        pltpu.SMEM((1, 2), jnp.int32), pltpu.SMEM((1, 1), jnp.int32),
        vmem(members * BLK, width), vmem(BLK, width), vmem(members * BLK, width), vmem(2 * BLK, width),
        vmem(rows, rows + (members + 2) * BLK),
        vmem(rows, width, dtype=F32), vmem(rows, width, dtype=F32),
        vmem(rows, width), vmem(rows, width),
        vmem(width, width), vmem(width, width), vmem(width, width, dtype=F32),
        vmem(width, width), vmem(width, width), vmem(chunk, width, dtype=F32),
        vmem(zs * piece, width), vmem(zs * piece, width), vmem(2 * width, width),
        vmem(members * BLK, width), vmem(members * BLK, width), vmem(2 * BLK, width), vmem(2 * BLK, width),
        dma((11,)), dma((3,)),
        dma((members,)), dma((members,)), dma((2,)), dma((2,)),
        dma((members,)), dma((members,)), dma((members,)), dma((members,)), dma((zs,)), dma((zs,)),
        dma((members,)), dma((members,)), dma((2,)), dma((2,)),
        dma((zs,)), dma((zs,)),
        dma((members * pieces,)), dma((members * pieces,)), dma((members * pieces,)), dma((members * pieces,)),
    ]
    output, feature_grads, grads = pl.pallas_call(
        functools.partial(kernel, domains, members, pieces, scale),
        out_shape=(
            jax.ShapeDtypeStruct((rows, width), BF16),
            jax.ShapeDtypeStruct((rows, width), BF16),
            jax.ShapeDtypeStruct((2 * width, width), BF16),
        ),
        in_specs=[any_space] * len(args),
        out_specs=(any_space,) * 3,
        scratch_shapes=scratch,
        compiler_params=pltpu.CompilerParams(
            collective_id=0, has_side_effects=True, vmem_limit_bytes=48 * 2**20
        ),
        name="sage_layer",
    )(*args)
    return output, feature_grads, grads[:width].astype(F32), grads[width:].astype(F32)


def solution(mesh):
    split = P(("dom", "rep"), None)
    split3 = P(("dom", "rep"), None, None)
    return jax.shard_map(
        functools.partial(body, mesh.shape["dom"], mesh.shape["rep"]),
        mesh=mesh,
        in_specs=(
            split, split, split3, split, split, split3, split, split, P(), P(), split,
        ),
        out_specs=(split, split, P(), P()),
        check_vma=False,
    )
```

time: 182 us -> 49.5 us (0.27)
  waiting for transfers between devices: 124 us -> 0 us
  Pallas kernels: 0 us -> 37.9 us
  starting transfers between devices: 19.7 us -> 0 us
  between operations: 15.2 us -> 1.38 us
  matrix products: 7.45 us -> 0 us
  other arithmetic: 5.4 us -> 1.6 us
    psum x2 -> x0, waiting for transfers between devices: 114 us -> none  [the longest x1 61.2 us: body(): group_self, group_neigh = lax.psum((self_part, neigh_part), 'rep')]
    pallas_call x0 -> x1, Pallas kernels: none -> 37.9 us  [body(): pl.pallas_call(functools.partial(kernel, domains, members, pieces, scale)...]
    ppermute x4 -> x0, starting transfers between devices: 12.5 us -> none  [the longest x2 7.65 us: with_halo(): lax.ppermute(tail, axis, [(i, (i + 1) % count) for i in range(ends)])]
    all_to_all x2 -> x0, waiting for transfers between devices: 10.5 us -> none  [the longest x1 6.17 us: body(): lax.all_to_all(edge_terms, 'rep', split_axis=0, concat_axis=0, tiled=True)]
    dot_general x15 -> x0, matrix products: 7.45 us -> none  [the longest x1 1.37 us: body(): jnp.dot(neighbour_mean, w_neigh, preferred_element_type=jnp.float32)]
    all_to_all x2 -> x0, starting transfers between devices: 7.09 us -> none  [the longest x1 3.62 us: body(): lax.all_to_all(outgoing, 'rep', split_axis=0, concat_axis=0, tiled=True)]
    unnamed x24 -> x22, local copies, waits for them, and re-layouts: 5.28 us -> 8.19 us
    select_n x5 -> x0, other arithmetic: 1.84 us -> none  [the longest x1 0.92 us: body(): exported = jnp.take(feat_blocks, export_block[0], axis=0)]
  transfers between devices with their start and end apart: 8 -> 0, of which waited for: 4 -> 0; matrix products, arithmetic and copies ran while one was open for 6% -> 0% of each run, Pallas kernels for 0% -> 0%
where the time goes in v1:
time: 49.5 us; the launch traced here: 49.1 us
  Pallas kernels  37.9 us (77%)
  local copies, waits for them, and re-layouts  8.19 us (17%)
  other arithmetic  1.6 us (3%)
  between operations  1.38 us (3%)
    pallas_call x1, Pallas kernels, body(): pl.pallas_call(functools.partial(kernel, domains, members, pieces, scale)...  37.9 us
    unnamed x22, local copies, waits for them, and re-layouts  8.19 us
    convert_element_type x1, other arithmetic, body(): grads[width:].astype(F32)  1.6 us

profile of v1, /device:TPU:1, one launch (start us, length us, event | category | flops | bytes accessed | tf_op | source)
XLA Modules:
  0.0 49.1 jit_solution(17004681172338405044)
XLA Ops:
  0.6 0.0 copy-start.9
  0.6 0.0 copy-start.8
  0.7 0.0 copy-start.7
  1.3 0.0 copy-done.9
  1.3 0.0 copy-done.8
  1.4 0.0 copy-done.7
  1.4 0.0 copy-start
  1.4 1.0 %copy-done = bf16[512,512]{1,0:T(8,128)(2,1)S(1)} copy-done((bf16[512,512]{1,0:T(8,128)(2,1)S(1)}, bf16[512,512]{1,0:T(8,128)(2,1)}, u32[]{:S(2)}) %copy-start) | copy-done | bytes 524312
  2.4 0.0 copy-start.1
  2.4 1.0 %copy-done.1 = bf16[512,512]{1,0:T(8,128)(2,1)S(1)} copy-done((bf16[512,512]{1,0:T(8,128)(2,1)S(1)}, bf16[512,512]{1,0:T(8,128)(2,1)}, u32[]{:S(2)}) %copy-start.1) | copy-done | bytes 524312
  3.5 0.0 copy-start.2
  3.5 0.9 %copy-done.2 = bf16[256,512]{1,0:T(8,128)(2,1)S(1)} copy-done((bf16[256,512]{1,0:T(8,128)(2,1)S(1)}, bf16[256,512]{1,0:T(8,128)(2,1)}, u32[]{:S(2)}) %copy-start.2) | copy-done | bytes 262168
  4.4 0.0 copy-start.3
  4.4 0.9 %copy-done.3 = s32[256,256]{1,0:T(8,128)S(1)} copy-done((s32[256,256]{1,0:T(8,128)S(1)}, s32[256,256]{1,0:T(8,128)}, u32[]{:S(2)}) %copy-start.3) | copy-done | bytes 262168
  5.4 0.0 copy-start.4
  5.4 0.9 %copy-done.4 = s32[4,128,128]{2,1,0:T(8,128)S(1)} copy-done((s32[4,128,128]{2,1,0:T(8,128)S(1)}, s32[4,128,128]{2,1,0:T(8,128)}, u32[]{:S(2)}) %copy-start.4) | copy-done | bytes 262168
  6.3 0.0 copy-start.5
  6.3 0.9 %copy-done.5 = bf16[256,512]{1,0:T(8,128)(2,1)S(1)} copy-done((bf16[256,512]{1,0:T(8,128)(2,1)S(1)}, bf16[256,512]{1,0:T(8,128)(2,1)}, u32[]{:S(2)}) %copy-start.5) | copy-done | bytes 262168
  7.3 0.0 copy-start.6
  7.3 0.9 %copy-done.6 = s32[2,128,128]{2,1,0:T(8,128)S(1)} copy-done((s32[2,128,128]{2,1,0:T(8,128)S(1)}, s32[2,128,128]{2,1,0:T(8,128)}, u32[]{:S(2)}) %copy-start.6) | copy-done | bytes 131096
  8.2 37.9 %sage_layer.1 = (bf16[256,512]{1,0:T(8,128)(2,1)S(1)}, bf16[256,512]{1,0:T(8,128)(2,1)S(1)}, bf16[1024,512]{1,0:T(8,128)(2,1)S(1)}) custom-call(bf16[256,512]{1,0:T(8,128)(2,1)S(1)} %copy-done.2, s32[256,256]{1,0:T(8,128)S(1)} %copy-done.3, s32[4,128,128]{2,1,0:T(8,128)S(1)} %copy-done.4, s32[1,4]{1,0:T(1,128)S(1)} %copy-done.7, s32[1,4]{1,0:T(1,128)S(1)} %copy-done.8, ...), custom_call_target="tpu_custom_call" | custom-call | tf_op jit(solution)/shard_map/sage_layer/pallas_call | solution.py:350
  46.1 1.6 %slice_convert_fusion = (f32[512,512]{1,0:T(8,128)}, f32[512,512]{1,0:T(8,128)}) fusion(bf16[1024,512]{1,0:T(8,128)(2,1)S(1)} %get-tuple-element.9), kind=kLoop, calls=%fused_computation | loop fusion | flops 524288 | bytes 3145728 | tf_op jit(solution)/shard_map/convert_element_type | solution.py:365
  47.7 0.7 %copy.18 = bf16[256,512]{1,0:T(8,128)(2,1)} copy(bf16[256,512]{1,0:T(8,128)(2,1)S(1)} %get-tuple-element.16) | data formatting | bytes 524288
  48.4 0.7 %copy.19 = bf16[256,512]{1,0:T(8,128)(2,1)} copy(bf16[256,512]{1,0:T(8,128)(2,1)S(1)} %get-tuple-element.17) | data formatting | bytes 524288
Async XLA Ops:
  0.6 0.7 %copy-start.9 = (s32[1,2]{1,0:T(1,128)S(1)}, s32[1,2]{1,0:T(1,128)}, u32[]{:S(2)}) copy-start(s32[1,2]{1,0:T(1,128)} %hdest_h.1) | copy-start | bytes 28
  0.6 0.7 %copy-start.8 = (s32[1,4]{1,0:T(1,128)S(1)}, s32[1,4]{1,0:T(1,128)}, u32[]{:S(2)}) copy-start(s32[1,4]{1,0:T(1,128)} %send_h.1) | copy-start | bytes 52
  0.7 0.7 %copy-start.7 = (s32[1,4]{1,0:T(1,128)S(1)}, s32[1,4]{1,0:T(1,128)}, u32[]{:S(2)}) copy-start(s32[1,4]{1,0:T(1,128)} %rdest_h.1) | copy-start | bytes 52
  1.4 1.0 %copy-start = (bf16[512,512]{1,0:T(8,128)(2,1)S(1)}, bf16[512,512]{1,0:T(8,128)(2,1)}, u32[]{:S(2)}) copy-start(bf16[512,512]{1,0:T(8,128)(2,1)} %ws_h.1) | copy-start | bytes 1572868
  2.4 1.0 %copy-start.1 = (bf16[512,512]{1,0:T(8,128)(2,1)S(1)}, bf16[512,512]{1,0:T(8,128)(2,1)}, u32[]{:S(2)}) copy-start(bf16[512,512]{1,0:T(8,128)(2,1)} %wn_h.1) | copy-start | bytes 1572868
  3.5 0.9 %copy-start.2 = (bf16[256,512]{1,0:T(8,128)(2,1)S(1)}, bf16[256,512]{1,0:T(8,128)(2,1)}, u32[]{:S(2)}) copy-start(bf16[256,512]{1,0:T(8,128)(2,1)} %feat_h.1) | copy-start | bytes 786436
  4.4 0.9 %copy-start.3 = (s32[256,256]{1,0:T(8,128)S(1)}, s32[256,256]{1,0:T(8,128)}, u32[]{:S(2)}) copy-start(s32[256,256]{1,0:T(8,128)} %loc_h.1) | copy-start | bytes 786436
  5.4 0.9 %copy-start.4 = (s32[4,128,128]{2,1,0:T(8,128)S(1)}, s32[4,128,128]{2,1,0:T(8,128)}, u32[]{:S(2)}) copy-start(s32[4,128,128]{2,1,0:T(8,128)} %rem_h.1) | copy-start | bytes 786436
  6.3 0.9 %copy-start.5 = (bf16[256,512]{1,0:T(8,128)(2,1)S(1)}, bf16[256,512]{1,0:T(8,128)(2,1)}, u32[]{:S(2)}) copy-start(bf16[256,512]{1,0:T(8,128)(2,1)} %cot_h.1) | copy-start | bytes 786436
  7.3 0.9 %copy-start.6 = (s32[2,128,128]{2,1,0:T(8,128)S(1)}, s32[2,128,128]{2,1,0:T(8,128)}, u32[]{:S(2)}) copy-start(s32[2,128,128]{2,1,0:T(8,128)} %halo_h.1) | copy-start | bytes 393220

commit v2 on v1

--- a/solution.py
+++ b/solution.py
@@ -37,7 +37,7 @@
     pair, loc_v, rem_v, halo_v, ws_v, wn_v, cot_v, out_v, fg_v,
     rdest, send, hdest, export,
     outgoing, exported, arrived, beside, adj, acc, lin, lg, mg,
-    mate_out, mate_in, own, xy_out, xy_in, zsum, z_out, z_in, grads,
+    mate_out, mate_in, own, xy_out, xy_in, z_out, z_in, grads,
     edge, returned, halo_edge, halo_back,
     in_sem, out_sem,
     f_send, f_recv, h_send, h_recv,
@@ -200,28 +200,34 @@
     out_copy = pltpu.make_async_copy(out_v, out_h, out_sem.at[0])
     out_copy.start()
 
+    layer = members * piece
+    parts = [(z + k) % zs for k in range(1, zs)] + [z] if pieces > 1 else [0]
+    mine = parts[-1]
     mate_out[...] = dot_t(pair[1 - core], lg[...]).astype(BF16)
-    order = peers + [me]
-    for q in order:
-        at = rows_at(q * chunk, chunk)
-        push(mate_out.at[at], mate_in.at[at], m_send.at[q], m_recv.at[q], (mate, me))
+
+    def mate_copy(j):
+        at = rows_at(j * layer, layer)
+        return mate_out.at[at], mate_in.at[at], m_send.at[j], m_recv.at[j], (mate, me)
+
+    for j in parts:
+        push(*mate_copy(j))
     own[...] = dot_t(pair[core], lg[...])
+    for n, j in enumerate(parts):
+        remote(*mate_copy(j)).wait_recv()
+        at = rows_at(j * layer, layer)
+        own[at, :] += mate_in[at, :].astype(F32)
+        xy_out[at, :] = own[at, :].astype(BF16)
+        for q in peers:
+            push(
+                xy_out.at[rows_at(j * layer + q * piece, piece)],
+                xy_in.at[rows_at((me * pieces + j) * piece, piece)],
+                x_send.at[q * pieces + j], x_recv.at[me * pieces + j], (dom, q),
+            )
 
     mg[...] = (dot_nt(lg[...], wn_v[...]) * inverse).astype(BF16)
     edge[...] = dot_t(adj[:, rows:rows + members * BLK], mg[...]).astype(BF16)
     halo_edge[...] = dot_t(adj[:, rows + members * BLK:], mg[...]).astype(BF16)
     returned[rows_at(me * BLK, BLK), :] = edge[rows_at(me * BLK, BLK), :]
-
-    for q in order:
-        at = rows_at(q * chunk, chunk)
-        remote(mate_out.at[at], mate_in.at[at], m_send.at[q], m_recv.at[q], (mate, me)).wait_recv()
-        both = own[at, :] + mate_in[at, :].astype(F32)
-        if q is me:
-            zsum[...] = both
-        else:
-            xy_out[at, :] = both.astype(BF16)
-            push(xy_out.at[at], xy_in.at[rows_at(me * chunk, chunk)], x_send.at[q], x_recv.at[me], (dom, q))
-
     for q in peers:
         push(
             edge.at[rows_at(q * BLK, BLK)], returned.at[rows_at(me * BLK, BLK)],
@@ -229,49 +235,83 @@
         )
     halo_b = exchange((halo_edge.at[pl.ds(0, BLK)], halo_edge.at[pl.ds(BLK, BLK)]), halo_back, b_send, b_recv)
     start_exchange(halo_b, halo_back)
-    acc[...] = dot_nt(lg[...], ws_v[...]) + dot_t(adj[:, :rows], mg[...])
-
-    for q in peers:
-        at = rows_at(q * chunk, chunk)
-        remote(xy_out.at[at], xy_in.at[at], x_send.at[q], x_recv.at[q], (dom, q)).wait_recv()
-        zsum[...] += xy_in[at, :].astype(F32)
-
-    def place(member, part):
-        return rows_at((core * members + member) * chunk + part * piece, piece)
 
     def z_slot(j):
         return z_in.at[rows_at(j * piece, piece)]
 
-    part = z if pieces > 1 else 0
-    for j in zpeers:
-        at = rows_at((j if pieces > 1 else 0) * piece, piece)
-        to = rows_at(j * piece, piece)
-        z_out[to, :] = zsum[at, :].astype(BF16)
-        push(z_out.at[to], z_slot(z), z_send.at[j], z_recv.at[z], (j * 2 + core, me))
-    z_in[rows_at(z * piece, piece), :] = zsum[rows_at(part * piece, piece), :].astype(BF16)
+    for j in parts:
+        total = own[rows_at(j * layer + me * piece, piece), :]
+        for q in peers:
+            slot = rows_at((q * pieces + j) * piece, piece)
+            remote(
+                xy_in.at[slot], xy_in.at[slot],
+                x_send.at[q * pieces + j], x_recv.at[q * pieces + j], (dom, q),
+            ).wait_recv()
+            total = total + xy_in[slot, :].astype(F32)
+        total = total.astype(BF16)
+        targets = [j] if pieces > 1 else zpeers
+        if pieces == 1 or j is not mine:
+            for to in targets:
+                out = rows_at(to * piece, piece)
+                z_out[out, :] = total
+                push(z_out.at[out], z_slot(z), z_send.at[to], z_recv.at[z], (to * 2 + core, me))
+        if j is mine:
+            z_in[rows_at(z * piece, piece), :] = total
+    acc[...] = dot_nt(lg[...], ws_v[...]) + dot_t(adj[:, :rows], mg[...])
     for j in zpeers:
         remote(z_slot(j), z_slot(j), z_send.at[j], z_recv.at[j], (j * 2 + core, me)).wait_recv()
     total = z_in[:piece, :].astype(F32)
     for j in range(1, zs):
         total = total + z_in[j * piece:(j + 1) * piece, :].astype(F32)
-    grads[place(me, part), :] = (total * scale).astype(BF16)
-
-    def spread(part):
-        at = grads.at[place(me, part)]
-        for q in peers:
-            push(at, at, gx_send.at[q * pieces + part], gx_recv.at[me * pieces + part], (dom, q))
-        push(at, at, gm_send.at[me * pieces + part], gm_recv.at[me * pieces + part], (mate, me))
+
+    def place(member, part, half=core):
+        return rows_at(half * width + part * layer + member * piece, piece)
+
+    grads[place(me, mine), :] = (total * scale).astype(BF16)
+
+    def to_mate(member, j):
+        at = grads.at[place(member, j)]
+        push(at, at, gm_send.at[member * pieces + j], gm_recv.at[member * pieces + j], (mate, me))
+
+    def to_peer(q, member, j):
+        at = grads.at[place(member, j)]
+        push(at, at, gx_send.at[q * pieces + j], gx_recv.at[member * pieces + j], (dom, q))
+
+    def from_peer(member, j):
+        at = grads.at[place(member, j)]
+        remote(at, at, gx_send.at[member * pieces + j], gx_recv.at[member * pieces + j], (dom, member)).wait_recv()
+
+    relay = members == 4
+    beside_x = me + 1 - 2 * (me % 2)
+    beside_y = (me + 2) % 4
+    direct = [beside_x, beside_y] if relay else peers
+
+    def spread(j):
+        for q in direct:
+            to_peer(q, me, j)
+        to_mate(me, j)
 
     if pieces > 1:
         at = grads.at[place(me, z)]
         for j in zpeers:
             push(at, at, gz_send.at[j], gz_recv.at[z], (j * 2 + core, me))
-    spread(part)
+    spread(mine)
     if pieces > 1:
         for j in zpeers:
             at = grads.at[place(me, j)]
             remote(at, at, gz_send.at[j], gz_recv.at[j], (j * 2 + core, me)).wait_recv()
             spread(j)
+
+    arrivals = [mine] + (zpeers if pieces > 1 else [])
+    for j in arrivals:
+        for q in direct:
+            from_peer(q, j)
+        if relay:
+            first = j % 2
+            source = beside_x * (1 - first) + beside_y * first
+            to_peer(beside_x + beside_y - source, source, j)
+        for q in direct:
+            to_mate(q, j)
 
     arrive_exchange(halo_b)
     for q in peers:
@@ -287,15 +327,14 @@
     fg_copy = pltpu.make_async_copy(fg_v, fg_h, out_sem.at[1])
     fg_copy.start()
 
-    parts = [part] + (zpeers if pieces > 1 else [])
-    for j in parts:
-        for q in peers:
-            at = grads.at[place(q, j)]
-            remote(at, at, gx_send.at[q * pieces + j], gx_recv.at[q * pieces + j], (dom, q)).wait_recv()
-            push(at, at, gm_send.at[q * pieces + j], gm_recv.at[q * pieces + j], (mate, me))
-    for j in parts:
-        for q in order:
-            at = grads.at[rows_at(((1 - core) * members + q) * chunk + j * piece, piece)]
+    if relay:
+        across = (beside_x + 2) % 4
+        for j in arrivals:
+            from_peer(across, j)
+            to_mate(across, j)
+    for j in arrivals:
+        for q in [me] + peers:
+            at = grads.at[place(q, j, 1 - core)]
             remote(at, at, gm_send.at[q * pieces + j], gm_recv.at[q * pieces + j], (mate, me)).wait_recv()
     grads_copy = pltpu.make_async_copy(grads, grads_h, out_sem.at[2])
     grads_copy.start()
@@ -307,6 +346,33 @@
     out_copy.wait()
     fg_copy.wait()
     grads_copy.wait()
+
+
+def finish(out_i, fg_i, grads_i, out_o, fg_o, self_o, neigh_o, narrow, wide, load_sem, sem):
+    width = self_o.shape[0]
+    loads = []
+    for start in range(0, 2 * width, BLK):
+        at = pl.ds(start, BLK)
+        loads.append(pltpu.make_async_copy(grads_i.at[at], narrow.at[at], load_sem.at[start // BLK]))
+        loads[-1].start()
+    copies = [
+        pltpu.make_async_copy(out_i, out_o, sem.at[0]),
+        pltpu.make_async_copy(fg_i, fg_o, sem.at[1]),
+    ]
+    for copy in copies:
+        copy.start()
+    for start in range(0, 2 * width, BLK):
+        at = pl.ds(start, BLK)
+        loads[start // BLK].wait()
+        wide[at, :] = narrow[at, :].astype(F32)
+        dst = self_o if start < width else neigh_o
+        copy = pltpu.make_async_copy(
+            wide.at[at], dst.at[pl.ds(start % width, BLK)], sem.at[2 + start // BLK]
+        )
+        copy.start()
+        copies.append(copy)
+    for copy in copies:
+        copy.wait()
 
 
 def body(domains, members, *args):
@@ -337,12 +403,12 @@
         vmem(rows, width, dtype=F32), vmem(rows, width, dtype=F32),
         vmem(rows, width), vmem(rows, width),
         vmem(width, width), vmem(width, width), vmem(width, width, dtype=F32),
-        vmem(width, width), vmem(width, width), vmem(chunk, width, dtype=F32),
+        vmem(width, width), vmem(width, width),
         vmem(zs * piece, width), vmem(zs * piece, width), vmem(2 * width, width),
         vmem(members * BLK, width), vmem(members * BLK, width), vmem(2 * BLK, width), vmem(2 * BLK, width),
         dma((11,)), dma((3,)),
         dma((members,)), dma((members,)), dma((2,)), dma((2,)),
-        dma((members,)), dma((members,)), dma((members,)), dma((members,)), dma((zs,)), dma((zs,)),
+        dma((pieces,)), dma((pieces,)), dma((members * pieces,)), dma((members * pieces,)), dma((zs,)), dma((zs,)),
         dma((members,)), dma((members,)), dma((2,)), dma((2,)),
         dma((zs,)), dma((zs,)),
         dma((members * pieces,)), dma((members * pieces,)), dma((members * pieces,)), dma((members * pieces,)),
@@ -358,11 +424,27 @@
         out_specs=(any_space,) * 3,
         scratch_shapes=scratch,
         compiler_params=pltpu.CompilerParams(
-            collective_id=0, has_side_effects=True, vmem_limit_bytes=48 * 2**20
+            collective_id=0, has_side_effects=True, vmem_limit_bytes=60 * 2**20
         ),
         name="sage_layer",
     )(*args)
-    return output, feature_grads, grads[:width].astype(F32), grads[width:].astype(F32)
+    return pl.pallas_call(
+        finish,
+        out_shape=(
+            jax.ShapeDtypeStruct((rows, width), BF16),
+            jax.ShapeDtypeStruct((rows, width), BF16),
+            jax.ShapeDtypeStruct((width, width), F32),
+            jax.ShapeDtypeStruct((width, width), F32),
+        ),
+        in_specs=[any_space] * 3,
+        out_specs=(any_space,) * 4,
+        scratch_shapes=[
+            vmem(2 * width, width), vmem(2 * width, width, dtype=F32),
+            dma((2 * width // BLK,)), dma((2 + 2 * width // BLK,)),
+        ],
+        compiler_params=pltpu.CompilerParams(vmem_limit_bytes=60 * 2**20),
+        name="finish",
+    )(output, feature_grads, grads)
 
 
 def solution(mesh):

time: 49.5 us -> 57 us (1.15)
  Pallas kernels: 37.9 us -> 55.6 us
  local copies, waits for them, and re-layouts: 8.19 us -> 0 us
  other arithmetic: 1.6 us -> 0 us
    pallas_call x0 -> x1, Pallas kernels: none -> 17.2 us  [body(): pl.pallas_call(finish, out_shape=(jax.ShapeDtypeStruct((rows, width), BF1...]
    unnamed x22 -> x0, local copies, waits for them, and re-layouts: 8.19 us -> none
    convert_element_type x1 -> x0, other arithmetic: 1.6 us -> none  [body(): grads[width:].astype(F32)]
where the time goes in v2:
time: 57 us; the launch traced here: 56.8 us
  Pallas kernels  55.6 us (98%)
  between operations  1.29 us (2%)
    pallas_call x1, Pallas kernels, body(): pl.pallas_call(functools.partial(kernel, domains, members, pieces, scale)...  38.4 us
    pallas_call x1, Pallas kernels, body(): pl.pallas_call(finish, out_shape=(jax.ShapeDtypeStruct((rows, width), BF1...  17.2 us

profile of v2, /device:TPU:1, one launch (start us, length us, event | category | flops | bytes accessed | tf_op | source)
XLA Modules:
  0.0 56.8 jit_solution(9458789370812194130)
XLA Ops:
  1.3 38.4 %sage_layer.1 = (bf16[256,512]{1,0:T(8,128)(2,1)}, bf16[256,512]{1,0:T(8,128)(2,1)}, bf16[1024,512]{1,0:T(8,128)(2,1)}) custom-call(bf16[256,512]{1,0:T(8,128)(2,1)} %feat_h.1, s32[256,256]{1,0:T(8,128)} %loc_h.1, s32[4,128,128]{2,1,0:T(8,128)} %rem_h.1, s32[1,4]{1,0:T(1,128)} %rdest_h.1, s32[1,4]{1,0:T(1,128)} %send_h.1, s32[2,128,128]{2,1,0:T(8,128)} %halo_h.1, ...), custom_call_target="tpu_custom_call" | custom-call | tf_op jit(solution)/shard_map/sage_layer/pallas_call | solution.py:416
  39.7 17.2 %finish.1 = (bf16[256,512]{1,0:T(8,128)(2,1)}, bf16[256,512]{1,0:T(8,128)(2,1)}, f32[512,512]{1,0:T(8,128)}, f32[512,512]{1,0:T(8,128)}) custom-call(bf16[256,512]{1,0:T(8,128)(2,1)} %get-tuple-element.7.out_i, bf16[256,512]{1,0:T(8,128)(2,1)} %get-tuple-element.8.fg_i, bf16[1024,512]{1,0:T(8,128)(2,1)} %get-tuple-element.9.grads_i), custom_call_target="tpu_custom_call" | custom-call | tf_op jit(solution)/shard_map/finish/pallas_call | solution.py:431

commit v3 on v2

--- a/solution.py
+++ b/solution.py
@@ -55,7 +55,11 @@
     blocks = rows // BLK
     chunk = width // members
     piece = chunk // pieces
-    peers = [(me + k) % members for k in range(1, members)]
+    relay = members == 4
+    beside_x = me + 1 - 2 * (me % 2)
+    beside_y = (me + 2) % 4
+    across = 3 - me
+    peers = [across, beside_x, beside_y] if relay else [(me + k) % members for k in range(1, members)]
     zpeers = [(z + k) % zs for k in range(1, zs)]
     has_prev = dom > 0
     has_next = dom < domains - 1
@@ -228,11 +232,6 @@
     edge[...] = dot_t(adj[:, rows:rows + members * BLK], mg[...]).astype(BF16)
     halo_edge[...] = dot_t(adj[:, rows + members * BLK:], mg[...]).astype(BF16)
     returned[rows_at(me * BLK, BLK), :] = edge[rows_at(me * BLK, BLK), :]
-    for q in peers:
-        push(
-            edge.at[rows_at(q * BLK, BLK)], returned.at[rows_at(me * BLK, BLK)],
-            e_send.at[q], e_recv.at[me], (dom, q),
-        )
     halo_b = exchange((halo_edge.at[pl.ds(0, BLK)], halo_edge.at[pl.ds(BLK, BLK)]), halo_back, b_send, b_recv)
     start_exchange(halo_b, halo_back)
 
@@ -257,6 +256,11 @@
                 push(z_out.at[out], z_slot(z), z_send.at[to], z_recv.at[z], (to * 2 + core, me))
         if j is mine:
             z_in[rows_at(z * piece, piece), :] = total
+    for q in peers:
+        push(
+            edge.at[rows_at(q * BLK, BLK)], returned.at[rows_at(me * BLK, BLK)],
+            e_send.at[q], e_recv.at[me], (dom, q),
+        )
     acc[...] = dot_nt(lg[...], ws_v[...]) + dot_t(adj[:, :rows], mg[...])
     for j in zpeers:
         remote(z_slot(j), z_slot(j), z_send.at[j], z_recv.at[j], (j * 2 + core, me)).wait_recv()
@@ -281,9 +285,6 @@
         at = grads.at[place(member, j)]
         remote(at, at, gx_send.at[member * pieces + j], gx_recv.at[member * pieces + j], (dom, member)).wait_recv()
 
-    relay = members == 4
-    beside_x = me + 1 - 2 * (me % 2)
-    beside_y = (me + 2) % 4
     direct = [beside_x, beside_y] if relay else peers
 
     def spread(j):
@@ -328,16 +329,24 @@
     fg_copy.start()
 
     if relay:
-        across = (beside_x + 2) % 4
         for j in arrivals:
             from_peer(across, j)
             to_mate(across, j)
+    writes = []
+
+    def write(half, j):
+        at = rows_at(half * width + j * layer, layer)
+        copy = pltpu.make_async_copy(grads.at[at], grads_h.at[at], out_sem.at[2 + len(writes)])
+        copy.start()
+        writes.append(copy)
+
+    for j in arrivals:
+        write(core, j)
     for j in arrivals:
         for q in [me] + peers:
             at = grads.at[place(q, j, 1 - core)]
             remote(at, at, gm_send.at[q * pieces + j], gm_recv.at[q * pieces + j], (mate, me)).wait_recv()
-    grads_copy = pltpu.make_async_copy(grads, grads_h, out_sem.at[2])
-    grads_copy.start()
+        write(1 - core, j)
 
     for copy in sends:
         copy.wait_send()
@@ -345,33 +354,36 @@
     end_exchange(halo_b)
     out_copy.wait()
     fg_copy.wait()
-    grads_copy.wait()
-
-
-def finish(out_i, fg_i, grads_i, out_o, fg_o, self_o, neigh_o, narrow, wide, load_sem, sem):
+    for copy in writes:
+        copy.wait()
+
+
+def finish(out_i, fg_i, grads_i, out_o, fg_o, self_o, neigh_o, out_v, fg_v, narrow, wide, load_sem, sem):
     width = self_o.shape[0]
-    loads = []
-    for start in range(0, 2 * width, BLK):
+    starts = range(0, 2 * width, BLK)
+    loads = [
+        pltpu.make_async_copy(grads_i.at[pl.ds(start, BLK)], narrow.at[pl.ds(start, BLK)], load_sem.at[2 + n])
+        for n, start in enumerate(starts)
+    ]
+    loads += [
+        pltpu.make_async_copy(out_i, out_v, load_sem.at[0]),
+        pltpu.make_async_copy(fg_i, fg_v, load_sem.at[1]),
+    ]
+    for copy in loads:
+        copy.start()
+    stores = []
+    for n, start in enumerate(starts):
         at = pl.ds(start, BLK)
-        loads.append(pltpu.make_async_copy(grads_i.at[at], narrow.at[at], load_sem.at[start // BLK]))
-        loads[-1].start()
-    copies = [
-        pltpu.make_async_copy(out_i, out_o, sem.at[0]),
-        pltpu.make_async_copy(fg_i, fg_o, sem.at[1]),
-    ]
-    for copy in copies:
-        copy.start()
-    for start in range(0, 2 * width, BLK):
-        at = pl.ds(start, BLK)
-        loads[start // BLK].wait()
+        loads[n].wait()
         wide[at, :] = narrow[at, :].astype(F32)
         dst = self_o if start < width else neigh_o
-        copy = pltpu.make_async_copy(
-            wide.at[at], dst.at[pl.ds(start % width, BLK)], sem.at[2 + start // BLK]
-        )
-        copy.start()
-        copies.append(copy)
-    for copy in copies:
+        stores.append(pltpu.make_async_copy(wide.at[at], dst.at[pl.ds(start % width, BLK)], sem.at[2 + n]))
+        stores[-1].start()
+    for n, (src, dst) in enumerate(((out_v, out_o), (fg_v, fg_o))):
+        loads[n - 2].wait()
+        stores.append(pltpu.make_async_copy(src, dst, sem.at[n]))
+        stores[-1].start()
+    for copy in stores:
         copy.wait()
 
 
@@ -406,7 +418,7 @@
         vmem(width, width), vmem(width, width),
         vmem(zs * piece, width), vmem(zs * piece, width), vmem(2 * width, width),
         vmem(members * BLK, width), vmem(members * BLK, width), vmem(2 * BLK, width), vmem(2 * BLK, width),
-        dma((11,)), dma((3,)),
+        dma((11,)), dma((2 + 2 * pieces,)),
         dma((members,)), dma((members,)), dma((2,)), dma((2,)),
         dma((pieces,)), dma((pieces,)), dma((members * pieces,)), dma((members * pieces,)), dma((zs,)), dma((zs,)),
         dma((members,)), dma((members,)), dma((2,)), dma((2,)),
@@ -439,8 +451,8 @@
         in_specs=[any_space] * 3,
         out_specs=(any_space,) * 4,
         scratch_shapes=[
-            vmem(2 * width, width), vmem(2 * width, width, dtype=F32),
-            dma((2 * width // BLK,)), dma((2 + 2 * width // BLK,)),
+            vmem(rows, width), vmem(rows, width), vmem(2 * width, width), vmem(2 * width, width, dtype=F32),
+            dma((2 + 2 * width // BLK,)), dma((2 + 2 * width // BLK,)),
         ],
         compiler_params=pltpu.CompilerParams(vmem_limit_bytes=60 * 2**20),
         name="finish",

time: 57 us -> 43.2 us (0.76)
  Pallas kernels: 55.6 us -> 41.7 us
    pallas_call x1, Pallas kernels: 17.2 us -> 2.58 us  [body(): pl.pallas_call(finish, out_shape=(jax.ShapeDtypeStruct((rows, width), BF1...]
    pallas_call x1, Pallas kernels: 38.4 us -> 39.1 us  [body(): pl.pallas_call(functools.partial(kernel, domains, members, pieces, scale)...]
where the time goes in v3:
time: 43.2 us; the launch traced here: 43 us
  Pallas kernels  41.7 us (97%)
  between operations  1.29 us (3%)
    pallas_call x1, Pallas kernels, body(): pl.pallas_call(functools.partial(kernel, domains, members, pieces, scale)...  39.1 us
    pallas_call x1, Pallas kernels, body(): pl.pallas_call(finish, out_shape=(jax.ShapeDtypeStruct((rows, width), BF1...  2.58 us

profile of v3, /device:TPU:1, one launch (start us, length us, event | category | flops | bytes accessed | tf_op | source)
XLA Modules:
  0.0 43.0 jit_solution(547670469218556196)
XLA Ops:
  1.3 39.1 %sage_layer.1 = (bf16[256,512]{1,0:T(8,128)(2,1)}, bf16[256,512]{1,0:T(8,128)(2,1)}, bf16[1024,512]{1,0:T(8,128)(2,1)}) custom-call(bf16[256,512]{1,0:T(8,128)(2,1)} %feat_h.1, s32[256,256]{1,0:T(8,128)} %loc_h.1, s32[4,128,128]{2,1,0:T(8,128)} %rem_h.1, s32[1,4]{1,0:T(1,128)} %rdest_h.1, s32[1,4]{1,0:T(1,128)} %send_h.1, s32[2,128,128]{2,1,0:T(8,128)} %halo_h.1, ...), custom_call_target="tpu_custom_call" | custom-call | tf_op jit(solution)/shard_map/sage_layer/pallas_call | solution.py:428
  40.4 2.6 %finish.1 = (bf16[256,512]{1,0:T(8,128)(2,1)}, bf16[256,512]{1,0:T(8,128)(2,1)}, f32[512,512]{1,0:T(8,128)}, f32[512,512]{1,0:T(8,128)}) custom-call(bf16[256,512]{1,0:T(8,128)(2,1)} %get-tuple-element.7.out_i, bf16[256,512]{1,0:T(8,128)(2,1)} %get-tuple-element.8.fg_i, bf16[1024,512]{1,0:T(8,128)(2,1)} %get-tuple-element.9.grads_i), custom_call_target="tpu_custom_call" | custom-call | tf_op jit(solution)/shard_map/finish/pallas_call | solution.py:443

commit v4 on v3

--- a/solution.py
+++ b/solution.py
@@ -314,6 +314,10 @@
         for q in direct:
             to_mate(q, j)
 
+    if relay:
+        for j in arrivals:
+            from_peer(across, j)
+            to_mate(across, j)
     arrive_exchange(halo_b)
     for q in peers:
         slot = returned.at[rows_at(q * BLK, BLK)]
@@ -328,10 +332,6 @@
     fg_copy = pltpu.make_async_copy(fg_v, fg_h, out_sem.at[1])
     fg_copy.start()
 
-    if relay:
-        for j in arrivals:
-            from_peer(across, j)
-            to_mate(across, j)
     writes = []
 
     def write(half, j):

time: 43.2 us -> 43.2 us (level)
  no operation moved by 1% of the time
where the time goes in v4:
time: 43.2 us; the launch traced here: 43 us
  Pallas kernels  41.7 us (97%)
  between operations  1.29 us (3%)
    pallas_call x1, Pallas kernels, body(): pl.pallas_call(functools.partial(kernel, domains, members, pieces, scale)...  39.1 us
    pallas_call x1, Pallas kernels, body(): pl.pallas_call(finish, out_shape=(jax.ShapeDtypeStruct((rows, width), BF1...  2.58 us

profile of v4, /device:TPU:1, one launch (start us, length us, event | category | flops | bytes accessed | tf_op | source)
XLA Modules:
  0.0 43.0 jit_solution(10375398873116783355)
XLA Ops:
  1.3 39.1 %sage_layer.1 = (bf16[256,512]{1,0:T(8,128)(2,1)}, bf16[256,512]{1,0:T(8,128)(2,1)}, bf16[1024,512]{1,0:T(8,128)(2,1)}) custom-call(bf16[256,512]{1,0:T(8,128)(2,1)} %feat_h.1, s32[256,256]{1,0:T(8,128)} %loc_h.1, s32[4,128,128]{2,1,0:T(8,128)} %rem_h.1, s32[1,4]{1,0:T(1,128)} %rdest_h.1, s32[1,4]{1,0:T(1,128)} %send_h.1, s32[2,128,128]{2,1,0:T(8,128)} %halo_h.1, ...), custom_call_target="tpu_custom_call" | custom-call | tf_op jit(solution)/shard_map/sage_layer/pallas_call | solution.py:428
  40.4 2.6 %finish.1 = (bf16[256,512]{1,0:T(8,128)(2,1)}, bf16[256,512]{1,0:T(8,128)(2,1)}, f32[512,512]{1,0:T(8,128)}, f32[512,512]{1,0:T(8,128)}) custom-call(bf16[256,512]{1,0:T(8,128)(2,1)} %get-tuple-element.7.out_i, bf16[256,512]{1,0:T(8,128)(2,1)} %get-tuple-element.8.fg_i, bf16[1024,512]{1,0:T(8,128)(2,1)} %get-tuple-element.9.grads_i), custom_call_target="tpu_custom_call" | custom-call | tf_op jit(solution)/shard_map/finish/pallas_call | solution.py:443

commit v5 on v4

--- a/solution.py
+++ b/solution.py
@@ -55,11 +55,10 @@
     blocks = rows // BLK
     chunk = width // members
     piece = chunk // pieces
-    relay = members == 4
     beside_x = me + 1 - 2 * (me % 2)
     beside_y = (me + 2) % 4
     across = 3 - me
-    peers = [across, beside_x, beside_y] if relay else [(me + k) % members for k in range(1, members)]
+    peers = [across, beside_x, beside_y] if members == 4 else [(me + k) % members for k in range(1, members)]
     zpeers = [(z + k) % zs for k in range(1, zs)]
     has_prev = dom > 0
     has_next = dom < domains - 1
@@ -285,10 +284,9 @@
         at = grads.at[place(member, j)]
         remote(at, at, gx_send.at[member * pieces + j], gx_recv.at[member * pieces + j], (dom, member)).wait_recv()
 
-    direct = [beside_x, beside_y] if relay else peers
 
     def spread(j):
-        for q in direct:
+        for q in peers:
             to_peer(q, me, j)
         to_mate(me, j)
 
@@ -305,19 +303,11 @@
 
     arrivals = [mine] + (zpeers if pieces > 1 else [])
     for j in arrivals:
-        for q in direct:
+        for q in peers:
             from_peer(q, j)
-        if relay:
-            first = j % 2
-            source = beside_x * (1 - first) + beside_y * first
-            to_peer(beside_x + beside_y - source, source, j)
-        for q in direct:
+        for q in peers:
             to_mate(q, j)
 
-    if relay:
-        for j in arrivals:
-            from_peer(across, j)
-            to_mate(across, j)
     arrive_exchange(halo_b)
     for q in peers:
         slot = returned.at[rows_at(q * BLK, BLK)]

time: 43.2 us -> 43.2 us (level)
  no operation moved by 1% of the time
where the time goes in v5:
time: 43.2 us; the launch traced here: 43 us
  Pallas kernels  41.7 us (97%)
  between operations  1.29 us (3%)
    pallas_call x1, Pallas kernels, body(): pl.pallas_call(functools.partial(kernel, domains, members, pieces, scale)...  39.1 us
    pallas_call x1, Pallas kernels, body(): pl.pallas_call(finish, out_shape=(jax.ShapeDtypeStruct((rows, width), BF1...  2.58 us

profile of v5, /device:TPU:1, one launch (start us, length us, event | category | flops | bytes accessed | tf_op | source)
XLA Modules:
  0.0 43.0 jit_solution(11849309216781248354)
XLA Ops:
  1.3 39.1 %sage_layer.1 = (bf16[256,512]{1,0:T(8,128)(2,1)}, bf16[256,512]{1,0:T(8,128)(2,1)}, bf16[1024,512]{1,0:T(8,128)(2,1)}) custom-call(bf16[256,512]{1,0:T(8,128)(2,1)} %feat_h.1, s32[256,256]{1,0:T(8,128)} %loc_h.1, s32[4,128,128]{2,1,0:T(8,128)} %rem_h.1, s32[1,4]{1,0:T(1,128)} %rdest_h.1, s32[1,4]{1,0:T(1,128)} %send_h.1, s32[2,128,128]{2,1,0:T(8,128)} %halo_h.1, ...), custom_call_target="tpu_custom_call" | custom-call | tf_op jit(solution)/shard_map/sage_layer/pallas_call | solution.py:418
  40.4 2.6 %finish.1 = (bf16[256,512]{1,0:T(8,128)(2,1)}, bf16[256,512]{1,0:T(8,128)(2,1)}, f32[512,512]{1,0:T(8,128)}, f32[512,512]{1,0:T(8,128)}) custom-call(bf16[256,512]{1,0:T(8,128)(2,1)} %get-tuple-element.7.out_i, bf16[256,512]{1,0:T(8,128)(2,1)} %get-tuple-element.8.fg_i, bf16[1024,512]{1,0:T(8,128)(2,1)} %get-tuple-element.9.grads_i), custom_call_target="tpu_custom_call" | custom-call | tf_op jit(solution)/shard_map/finish/pallas_call | solution.py:433
